TPU v7x, 32 devices: a whole 2x2x4 slice. The times are simulated.
32 devices in a mesh: ctx: 8 (over z, y), rep: 4 (over x, core).
Axes of the slice: x: 2, y: 2, z: 4, core: 2. Of those that a mesh axis runs over, the one named last changes fastest.
Arguments:
- queries: bfloat16 [4096, 1024], P(('rep', 'ctx')), parts along dimension 0, may hold values from -6 to 6
- key_rows: bfloat16 [4096, 1024], P(('rep', 'ctx')), parts along dimension 0, may hold values from -6 to 6
- value_rows: bfloat16 [4096, 1024], P(('rep', 'ctx')), parts along dimension 0, may hold values from -8 to 8
- doc_blocks: int32 [12], P('rep'), parts along dimension 0, may hold values from 1 to 4, 8 in all
- phm_mix: float32 [4, 4, 4], replicated, may hold values from -4 to 4
- phm_blocks: bfloat16 [1024, 1280], P('ctx'), may hold values from -0.1875 to 0.1875
Outputs:
- projected: bfloat16 [4096, 5120], P(('rep', 'ctx')), parts along dimension 0
There are 4 independent parts, one for each index of `rep`. A program takes and returns all parts, laid end to end along the dimension named above; an argument that names none is the same for every part. Nothing has to cross between parts.
Inputs may be any that keep to these rules, and one draw needn't show every extreme that they name: `doc_blocks`: entries sum to 8; the largest entry is exactly 4.
All inputs are finite; a program needn't handle non-finite values.
Results may differ from a plain program's by a relative error of at most 0.006.
Values may be sent and summed in bfloat16 or wider, within the bound.
A program may use at most 64 MiB of HBM per device.

v0:
```python
import math

import jax
import jax.numpy as jnp
from jax import lax
from jax.sharding import PartitionSpec as P

HEAD_DIM = 128
PHM_N = 4
UNIT = 128


def attend(q_all, k_all, v_all, doc_ids):
    seq_len = q_all.shape[0]
    block = min(512, seq_len)
    count = seq_len // block
    scale = 1.0 / math.sqrt(HEAD_DIM)
    heads_here = q_all.shape[1]

    def query_block(which):
        anchor = which * block
        q_part = lax.dynamic_slice_in_dim(q_all, anchor, block, 0)
        q_docs = lax.dynamic_slice_in_dim(doc_ids, anchor, block, 0)
        q_pos = anchor + jnp.arange(block, dtype=jnp.int32)
        lowest = jnp.int32(0)

        def key_block(kb, carry):
            running, total, accum = carry
            k_part = lax.dynamic_slice_in_dim(k_all, kb * block, block, 0)
            v_part = lax.dynamic_slice_in_dim(v_all, kb * block, block, 0)
            k_docs = lax.dynamic_slice_in_dim(doc_ids, kb * block, block, 0)
            k_pos = kb * block + jnp.arange(block, dtype=jnp.int32)
            allowed = (k_pos[None, :] <= q_pos[:, None]) & (k_docs[None, :] == q_docs[:, None])
            scores = (
                jnp.einsum("qhe,khe->hqk", q_part, k_part, preferred_element_type=jnp.float32)
                * scale
            )
            scores = jnp.where(allowed[None], scores, -1e30)
            newest = jnp.maximum(running, jnp.max(scores, axis=2))
            factor = jnp.exp(running - newest)
            expd = jnp.where(allowed[None], jnp.exp(scores - newest[:, :, None]), 0.0)
            total = total * factor + jnp.sum(expd, axis=2)
            update = jnp.einsum(
                "hqk,khe->hqe",
                expd.astype(jnp.bfloat16),
                v_part,
                preferred_element_type=jnp.float32,
            )
            accum = accum * factor[:, :, None] + update
            return (newest, total, accum)

        start_carry = (
            jnp.full((heads_here, block), -1e30, jnp.float32),
            jnp.zeros((heads_here, block), jnp.float32),
            jnp.zeros((heads_here, block, HEAD_DIM), jnp.float32),
        )
        running, total, accum = lax.fori_loop(lowest, which + 1, key_block, start_carry)
        result = (accum / total[:, :, None]).astype(jnp.bfloat16)
        return result.transpose(1, 0, 2)

    blocks_out = lax.map(query_block, jnp.arange(count, dtype=jnp.int32))
    return blocks_out.reshape(seq_len, heads_here, HEAD_DIM)


def body(queries, key_rows, value_rows, doc_blocks, phm_mix, phm_blocks):
    tok_rows = queries.shape[0]
    heads = queries.shape[1] // HEAD_DIM
    shaped = (
        queries.reshape(tok_rows, heads, HEAD_DIM),
        key_rows.reshape(tok_rows, heads, HEAD_DIM),
        value_rows.reshape(tok_rows, heads, HEAD_DIM),
    )
    q_all, k_all, v_all = (
        lax.all_to_all(shaped[0], "ctx", split_axis=1, concat_axis=0, tiled=True),
        lax.all_to_all(shaped[1], "ctx", split_axis=1, concat_axis=0, tiled=True),
        lax.all_to_all(shaped[2], "ctx", split_axis=1, concat_axis=0, tiled=True),
    )
    seq_len = q_all.shape[0]
    lengths = doc_blocks * UNIT
    ends = jnp.cumsum(lengths)
    positions = jnp.arange(seq_len, dtype=jnp.int32)
    doc_ids = jnp.sum((positions[:, None] >= ends[None, :]).astype(jnp.int32), axis=1)
    attended = attend(q_all, k_all, v_all, doc_ids)
    returned = lax.all_to_all(attended, "ctx", split_axis=0, concat_axis=1, tiled=True)
    rows_phm = heads * HEAD_DIM // PHM_N
    pieces = returned.reshape(tok_rows, PHM_N, rows_phm).astype(jnp.float32)
    mixed = jnp.einsum("iab,tar->tbir", phm_mix, pieces, precision=lax.Precision.HIGHEST)
    mixed = mixed.astype(jnp.bfloat16).reshape(tok_rows, PHM_N, PHM_N * rows_phm)
    cols_phm = phm_blocks.shape[1]
    output = jnp.einsum(
        "tbk,kc->tbc",
        mixed,
        lax.all_gather(phm_blocks, "ctx", axis=0, tiled=True),
        preferred_element_type=jnp.float32,
    )
    return output.reshape(tok_rows, PHM_N * cols_phm).astype(jnp.bfloat16)


def solution(mesh):
    placed = (
        P(("rep", "ctx"), None),
        P(("rep", "ctx"), None),
        P(("rep", "ctx"), None),
        P("rep"),
        P(),
        P("ctx", None),
    )
    return jax.shard_map(
        body, mesh=mesh, in_specs=placed, out_specs=P(("rep", "ctx"), None), check_vma=False
    )
```

profile of v0, /device:TPU:0, one launch (start us, length us, event | category | flops | bytes accessed | tf_op | source)
XLA Modules:
  0.0 114.4 jit_solution(4855069807807212398)
XLA Ops:
  6.5 1.8 %copy.56 = bf16[128,1024]{0,1:T(8,128)(2,1)} copy(bf16[128,1024]{1,0:T(8,128)(2,1)} %param.11) | data formatting | bytes 524288 | tf_op args[1]
  8.4 7.3 %all-to-all-start.1 = ((bf16[128,8,128]{0,2,1:T(8,128)(2,1)}), bf16[128,8,128]{0,2,1:T(8,128)(2,1)S(1)}, u32[]{:S(2)}, u32[]{:S(2)}) async-start(bf16[128,8,128]{0,2,1:T(8,128)(2,1)} %bitcast.10), calls=%async_computation.1 | async-start | bytes 524288 | tf_op jit(solution)/shard_map/all_to_all | solution.py:75
  15.6 1.8 %copy.58 = bf16[128,1024]{0,1:T(8,128)(2,1)} copy(bf16[128,1024]{1,0:T(8,128)(2,1)} %param.12) | data formatting | bytes 524288 | tf_op args[2]
  17.4 7.1 %all-to-all-done.1 = bf16[128,8,128]{0,2,1:T(8,128)(2,1)S(1)} async-done(((bf16[128,8,128]{0,2,1:T(8,128)(2,1)}), bf16[128,8,128]{0,2,1:T(8,128)(2,1)S(1)}, u32[]{:S(2)}, u32[]{:S(2)}) %all-to-all-start.1) | async-done | bytes 262176 | tf_op jit(solution)/shard_map/all_to_all | solution.py:75
  24.6 3.6 %all-to-all-start.2 = ((bf16[128,8,128]{0,2,1:T(8,128)(2,1)}), bf16[128,8,128]{0,2,1:T(8,128)(2,1)S(1)}, u32[]{:S(2)}, u32[]{:S(2)}) async-start(bf16[128,8,128]{0,2,1:T(8,128)(2,1)} %bitcast.14), calls=%async_computation.2 | async-start | bytes 524288 | tf_op jit(solution)/shard_map/all_to_all | solution.py:76
  28.1 1.8 %copy.54 = bf16[128,1024]{0,1:T(8,128)(2,1)} copy(bf16[128,1024]{1,0:T(8,128)(2,1)} %param.10) | data formatting | bytes 524288 | tf_op args[0]
  29.9 6.8 %all-to-all-done.2 = bf16[128,8,128]{0,2,1:T(8,128)(2,1)S(1)} async-done(((bf16[128,8,128]{0,2,1:T(8,128)(2,1)}), bf16[128,8,128]{0,2,1:T(8,128)(2,1)S(1)}, u32[]{:S(2)}, u32[]{:S(2)}) %all-to-all-start.2) | async-done | bytes 262176 | tf_op jit(solution)/shard_map/all_to_all | solution.py:76
  36.7 3.6 %all-to-all-start = ((bf16[128,8,128]{0,2,1:T(8,128)(2,1)}), bf16[128,8,128]{0,2,1:T(8,128)(2,1)S(1)}, u32[]{:S(2)}, u32[]{:S(2)}) async-start(bf16[128,8,128]{0,2,1:T(8,128)(2,1)} %bitcast.6), calls=%async_computation | async-start | bytes 524288 | tf_op jit(solution)/shard_map/all_to_all | solution.py:74
  40.3 0.7 all-gather.2.cloned.1.call-update
  41.1 0.2 reduce-window.8
  41.2 0.1 convert_reduce_fusion
  41.3 0.2 copy.57
  41.5 0.2 copy.59
  41.7 7.1 %all-to-all-done = bf16[128,8,128]{0,2,1:T(8,128)(2,1)S(1)} async-done(((bf16[128,8,128]{0,2,1:T(8,128)(2,1)}), bf16[128,8,128]{0,2,1:T(8,128)(2,1)S(1)}, u32[]{:S(2)}, u32[]{:S(2)}) %all-to-all-start) | async-done | bytes 262176 | tf_op jit(solution)/shard_map/all_to_all | solution.py:74
  48.8 0.2 copy.55
  49.0 9.1 %while.26 = (s32[]{:T(128)}, bf16[2,512,1,128]{3,1,2,0:T(8,128)(2,1)S(1)}, s32[2]{0:T(128)S(1)}, s32[1024]{0:T(1024)S(1)}, bf16[1024,1,128]{2,0,1:T(8,128)(2,1)S...) while((s32[]{:T(128)}, ...), condition=%wide.region_7.8_spmd, body=%wide.region_2.7_spmd.sunk | while | flops 139200512 | bytes 5057106 | solution.py:61
  49.0 0.6 dynamic_slice.40
  50.4 0.1 dynamic_slice.41
  51.2 1.5 %while.27 = (s32[]{:T(128)}, f32[1,512]{1,0:T(1,128)S(1)}, f32[1,512]{1,0:T(1,128)S(1)}, f32[1,512,128]{2,1,0:T(8,128)S(1)}, s32[]{:T(128)}, /*index=5*/s32[1024...) while((s32[]{:T(128)}, f32[1,512]{1,0:T(1,128)S(1)}, ...), condition=%wide.region_6.6_spmd.clone, body=%wide.region_3.5_spmd.clone.sunk | while | flops 139069440 | bytes 4128975 | solution.py:57
  51.2 0.1 dynamic_slice.44
  51.3 0.4 fusion.35
  51.7 0.3 fusion.36
  52.0 0.6 fusion.37
  52.7 0.2 bitcast_dynamic-update-slice_fusion.2
  52.9 0.6 dynamic_slice.40
  54.2 0.1 dynamic_slice.41
  55.0 3.0 %while.27 = (s32[]{:T(128)}, f32[1,512]{1,0:T(1,128)S(1)}, f32[1,512]{1,0:T(1,128)S(1)}, f32[1,512,128]{2,1,0:T(8,128)S(1)}, s32[]{:T(128)}, /*index=5*/s32[1024...) while((s32[]{:T(128)}, f32[1,512]{1,0:T(1,128)S(1)}, ...), condition=%wide.region_6.6_spmd.clone, body=%wide.region_3.5_spmd.clone.sunk | while | flops 139069440 | bytes 4128975 | solution.py:57
  55.0 0.1 dynamic_slice.44
  55.1 0.4 fusion.35
  55.5 0.3 fusion.36
  55.9 0.6 fusion.37
  56.5 0.1 dynamic_slice.44
  56.6 0.4 fusion.35
  57.0 0.3 fusion.36
  57.3 0.6 fusion.37
  58.0 0.2 bitcast_dynamic-update-slice_fusion.2
  58.2 0.5 broadcast.35
  58.7 0.8 reduce.4
  59.6 13.9 %all_to_all.69 = bf16[8,2,8192]{2,1,0:T(2,128)(2,1)S(1)} all-to-all(bf16[8,2,8192]{2,1,0:T(2,128)(2,1)S(1)} %reshape.102), channel_id=1, replica_groups=mesh['ctx'=8,'rep'=4] {'ctx'}, dimensions={0} | all-to-all | bytes 524288 | tf_op jit(solution)/shard_map/all_to_all | solution.py:84
  73.5 0.3 reshape.103
  73.8 0.2 copy.61
  74.0 0.2 reshape.98
  74.1 1.8 %fusion.23 = bf16[128,4,4,256]{3,1,2,0:T(4,128)(2,1)S(1)} fusion(bf16[128,4,256,1]{2,1,0,3:T(4,128)(2,1)S(1)} %reshape.98, f32[4,4,4]{2,1,0:T(4,128)S(1)} %copy-done), kind=kOutput, calls=%fused_computation.34 | convolution fusion | flops 25690112 | bytes 1310976 | tf_op jit(solution)/shard_map/iab,tar->tbir/dot_general | solution.py:87
  76.0 1.0 copy.63
  77.0 25.1 %all-gather.2.cloned.1.call-done = bf16[1024,1280]{1,0:T(8,128)(2,1)} async-done(((bf16[128,1280]{1,0:T(8,128)(2,1)}), bf16[1024,1280]{1,0:T(8,128)(2,1)}) %all-gather.2.cloned.1.call-update) | async-done | bytes 2621456 | tf_op jit(solution)/shard_map/all_gather | solution.py:93
  102.0 3.3 %convolution_convert_fusion = bf16[128,4,1280]{2,0,1:T(8,128)(2,1)S(1)} fusion(bf16[128,4,1024]{0,2,1:T(8,128)(2,1)S(1)} %bitcast.98, bf16[1024,1280]{1,0:T(8,128)(2,1)} %all-gather.2.cloned.1.call-done), kind=kOutput, calls=%fused_computation.31 | convolution fusion | flops 1342832640 | bytes 4980736 | tf_op jit(solution)/shard_map/tbk,kc->tbc/dot_general | solution.py:90
  105.4 0.8 copy.65
  106.2 1.4 %copy.66 = bf16[128,5120]{1,0:T(8,128)(2,1)} copy(bf16[128,5120]{0,1:T(8,128)(2,1)S(1)} %bitcast.96) | data formatting | bytes 2621440 | tf_op jit(solution)/shard_map/convert_element_type | solution.py:96
  (30 shorter events, 0.3 us)
Async XLA Ops:
  6.5 67.6 %copy-start = (f32[4,4,4]{2,1,0:T(4,128)S(1)}, f32[4,4,4]{2,1,0:T(4,128)}, u32[]{:S(2)}) copy-start(f32[4,4,4]{2,1,0:T(4,128)} %param.14) | copy-start | bytes 772
  6.5 34.5 %copy-start.1 = (s32[3]{0:T(128)S(1)}, s32[3]{0:T(128)}, u32[]{:S(2)}) copy-start(s32[3]{0:T(128)} %param.13) | copy-start | bytes 40
  8.4 16.2 %all-to-all-start.1 = ((bf16[128,8,128]{0,2,1:T(8,128)(2,1)}), bf16[128,8,128]{0,2,1:T(8,128)(2,1)S(1)}, u32[]{:S(2)}, u32[]{:S(2)}) async-start(bf16[128,8,128]{0,2,1:T(8,128)(2,1)} %bitcast.10), calls=%async_computation.1 | async-start | bytes 524288 | tf_op jit(solution)/shard_map/all_to_all | solution.py:75
  24.6 12.2 %all-to-all-start.2 = ((bf16[128,8,128]{0,2,1:T(8,128)(2,1)}), bf16[128,8,128]{0,2,1:T(8,128)(2,1)S(1)}, u32[]{:S(2)}, u32[]{:S(2)}) async-start(bf16[128,8,128]{0,2,1:T(8,128)(2,1)} %bitcast.14), calls=%async_computation.2 | async-start | bytes 524288 | tf_op jit(solution)/shard_map/all_to_all | solution.py:76
  36.7 12.1 %all-to-all-start = ((bf16[128,8,128]{0,2,1:T(8,128)(2,1)}), bf16[128,8,128]{0,2,1:T(8,128)(2,1)S(1)}, u32[]{:S(2)}, u32[]{:S(2)}) async-start(bf16[128,8,128]{0,2,1:T(8,128)(2,1)} %bitcast.6), calls=%async_computation | async-start | bytes 524288 | tf_op jit(solution)/shard_map/all_to_all | solution.py:74
  40.3 61.7 %all-gather.2.cloned.1.call-start = ((), (), s32[]{:S(2)}) async-start(), calls=%async_computation.4 | async-start | bytes 2949120 | tf_op jit(solution)/shard_map/all_gather | solution.py:93
Sparse Core Ops, SparseCore 0:
  43.3 58.6 all-gather.1
where the time goes:
time: 115 us; the launch traced here: 114 us
  waiting for transfers between devices  46.8 us (41%)
  starting transfers between devices  14.5 us (13%)
  blocking collectives  13.9 us (12%)
  between operations  13.5 us (12%)
  local copies, waits for them, and re-layouts  12.2 us (11%)
  matrix products  8.15 us (7%)
  loops' own time  2.99 us (3%)
  other arithmetic  2.46 us (2%)
    all_gather x1, waiting for transfers between devices, body(): lax.all_gather(phm_blocks, 'ctx', axis=0, tiled=True)  25.1 us
    all_to_all x1, blocking collectives, body(): lax.all_to_all(attended, 'ctx', split_axis=0, concat_axis=1, tiled=True)  13.9 us
    all_to_all x1, starting transfers between devices, body(): lax.all_to_all(shaped[1], 'ctx', split_axis=1, concat_axis=0, tiled=True)  7.28 us
    all_to_all x1, waiting for transfers between devices, body(): lax.all_to_all(shaped[1], 'ctx', split_axis=1, concat_axis=0, tiled=True)  7.14 us
    all_to_all x1, waiting for transfers between devices, body(): lax.all_to_all(shaped[0], 'ctx', split_axis=1, concat_axis=0, tiled=True)  7.1 us
    all_to_all x1, waiting for transfers between devices, body(): lax.all_to_all(shaped[2], 'ctx', split_axis=1, concat_axis=0, tiled=True)  6.78 us
    unnamed x10, local copies, waits for them, and re-layouts  5.75 us
    all_to_all x1, starting transfers between devices, body(): lax.all_to_all(shaped[0], 'ctx', split_axis=1, concat_axis=0, tiled=True)  3.59 us
  transfers between devices with their start and end apart: 4, of which 4 were waited for; matrix products, arithmetic and copies ran while one was open for 13% of the time, Pallas kernels for 0%

commit v1 on v0

--- a/solution.py
+++ b/solution.py
@@ -1,8 +1,11 @@
+import functools
 import math
 
 import jax
 import jax.numpy as jnp
 from jax import lax
+from jax.experimental import pallas as pl
+from jax.experimental.pallas import tpu as pltpu
 from jax.sharding import PartitionSpec as P
 
 HEAD_DIM = 128
@@ -96,6 +99,309 @@
     return output.reshape(tok_rows, PHM_N * cols_phm).astype(jnp.bfloat16)
 
 
+MESH = pl.DeviceIdType.MESH
+ROWS = UNIT
+MASKED = -1e30
+
+
+def fused_kernel(
+    docs_ref, mix_ref, q_ref, k_ref, v_ref, w_ref, out_ref,
+    qkv, obuf, att, wbuf, mixed,
+    qkv_send, qkv_recv, o_send, o_recv, w_send, w_recv, own_sem,
+):
+    ctx = 8
+    window = 4
+    d = lax.axis_index("ctx")
+    r = lax.axis_index("rep")
+    z = d // 2
+    y_peer = d + 1 - 2 * (d % 2)
+    x_peer = (r + 2) % 4
+    c_peer = r + 1 - 2 * (r % 2)
+    part = ROWS // 4
+
+    barrier = pltpu.get_barrier_semaphore()
+    for off in range(1, ctx):
+        pl.semaphore_signal(
+            barrier, inc=1, device_id={"ctx": (d + off) % ctx}, device_id_type=MESH
+        )
+    for peer in (x_peer, c_peer):
+        pl.semaphore_signal(barrier, inc=1, device_id={"rep": peer}, device_id_type=MESH)
+    pl.semaphore_wait(barrier, ctx + 1)
+
+    def quarter(shard, which):
+        return wbuf.at[shard, pl.ds(pl.multiple_of(which * part, part), part)]
+
+    def w_copy(src, shard, which, way, target):
+        return pltpu.make_async_remote_copy(
+            src_ref=src,
+            dst_ref=quarter(shard, which),
+            send_sem=w_send.at[way, shard, which],
+            recv_sem=w_recv.at[shard, which],
+            device_id=target,
+            device_id_type=MESH,
+        )
+
+    def w_arrived(shard, which):
+        here = quarter(shard, which)
+        pltpu.make_async_copy(here, here, w_recv.at[shard, which]).wait()
+
+    def w_sent(shard, which, way):
+        here = quarter(shard, which)
+        pltpu.make_async_copy(here, here, w_send.at[way, shard, which]).wait()
+
+    own_w = w_ref.at[pl.ds(pl.multiple_of(r * part, part), part)]
+
+    @pl.when(z < 3)
+    def _():
+        w_copy(own_w, d, r, 0, {"ctx": d + 2}).start()
+
+    @pl.when(z > 0)
+    def _():
+        w_copy(own_w, d, r, 1, {"ctx": d - 2}).start()
+
+    w_copy(own_w, d, r, 2, {"ctx": y_peer}).start()
+
+    refs = (q_ref, k_ref, v_ref)
+
+    def head_copy(j, to):
+        return pltpu.make_async_remote_copy(
+            src_ref=refs[j].at[:, pl.ds(pl.multiple_of(to * HEAD_DIM, HEAD_DIM), HEAD_DIM)],
+            dst_ref=qkv.at[j, d],
+            send_sem=qkv_send.at[j, to],
+            recv_sem=qkv_recv.at[j, d],
+            device_id={"ctx": to},
+            device_id_type=MESH,
+        )
+
+    for off in (4, 5, 3, 6, 2, 7, 1):
+        for j in range(3):
+            head_copy(j, (d + off) % ctx).start()
+    for j in range(3):
+        pltpu.make_async_copy(
+            refs[j].at[:, pl.ds(pl.multiple_of(d * HEAD_DIM, HEAD_DIM), HEAD_DIM)],
+            qkv.at[j, d],
+            qkv_recv.at[j, d],
+        ).start()
+    own_copy = pltpu.make_async_copy(w_ref, wbuf.at[d], own_sem)
+    own_copy.start()
+
+    def forward(shard, which, way, target):
+        w_copy(quarter(shard, which), shard, which, way, target).start()
+
+    for k in range(1, 4):
+
+        @pl.when(z - k >= 0)
+        def _():
+            shard = d - 2 * k
+            w_arrived(shard, r)
+
+            @pl.when(z < 3)
+            def _():
+                forward(shard, r, 0, {"ctx": d + 2})
+
+            forward(shard, r, 2, {"ctx": y_peer})
+            forward(shard, r, 3, {"rep": x_peer})
+            forward(shard, r, 4, {"rep": c_peer})
+
+        @pl.when(z + k <= 3)
+        def _():
+            shard = d + 2 * k
+            w_arrived(shard, r)
+
+            @pl.when(z > 0)
+            def _():
+                forward(shard, r, 1, {"ctx": d - 2})
+
+            forward(shard, r, 2, {"ctx": y_peer})
+            forward(shard, r, 3, {"rep": x_peer})
+            forward(shard, r, 4, {"rep": c_peer})
+
+    for k in range(4):
+        shard = (y_peer + 2 * k) % ctx
+        w_arrived(shard, r)
+        forward(shard, r, 3, {"rep": x_peer})
+        forward(shard, r, 4, {"rep": c_peer})
+
+    ends = [docs_ref[0]]
+    for i in range(1, docs_ref.shape[0]):
+        ends.append(ends[-1] + docs_ref[i])
+    ids = []
+    for b in range(ctx):
+        doc = jnp.int32(0)
+        for e in ends:
+            doc = doc + jnp.where(e <= b, jnp.int32(1), jnp.int32(0))
+        ids.append(doc)
+    factor = math.log2(math.e) / math.sqrt(HEAD_DIM)
+    rows = lax.broadcasted_iota(jnp.int32, (ROWS, ROWS), 0)
+    cols = lax.broadcasted_iota(jnp.int32, (ROWS, ROWS), 1)
+
+    def o_copy(b):
+        return pltpu.make_async_remote_copy(
+            src_ref=obuf.at[b],
+            dst_ref=att.at[d],
+            send_sem=o_send.at[b],
+            recv_sem=o_recv.at[d],
+            device_id={"ctx": b},
+            device_id_type=MESH,
+        )
+
+    for b in range(ctx):
+        for j in range(3):
+            here = qkv.at[j, b]
+            pltpu.make_async_copy(here, here, qkv_recv.at[j, b]).wait()
+        low = max(0, b - window + 1)
+        wide = (b + 1 - low) * ROWS
+        keys = qkv[1, low : b + 1].reshape(wide, HEAD_DIM)
+        vals = qkv[2, low : b + 1].reshape(wide, HEAD_DIM)
+        scores = lax.dot_general(
+            qkv[0, b], keys, (((1,), (1,)), ((), ())), preferred_element_type=jnp.float32
+        )
+        parts = []
+        for kb in range(low, b + 1):
+            one = scores[:, (kb - low) * ROWS : (kb - low + 1) * ROWS]
+            if kb == b:
+                one = jnp.where(cols <= rows, one, MASKED)
+            else:
+                one = one + jnp.where(ids[kb] == ids[b], 0.0, MASKED)
+            parts.append(one)
+        masked = jnp.concatenate(parts, axis=1) if len(parts) > 1 else parts[0]
+        top = jnp.max(masked, axis=1, keepdims=True)
+        expd = jnp.exp2((masked - top) * factor)
+        total = jnp.sum(expd, axis=1, keepdims=True)
+        got = jnp.dot(expd.astype(jnp.bfloat16), vals, preferred_element_type=jnp.float32)
+        obuf[b] = (got / total).astype(jnp.bfloat16)
+
+        @pl.when(d != b)
+        def _():
+            o_copy(b).start()
+
+        @pl.when(d == b)
+        def _():
+            pltpu.make_async_copy(obuf.at[b], att.at[d], o_recv.at[d]).start()
+
+    for off in range(1, ctx):
+        shard = (d + off) % ctx
+        w_arrived(shard, x_peer)
+        forward(shard, x_peer, 4, {"rep": c_peer})
+
+    for h in range(ctx):
+        here = att.at[h]
+        pltpu.make_async_copy(here, here, o_recv.at[h]).wait()
+
+    for half in range(2):
+        pieces = [att[2 * a + half].astype(jnp.float32) for a in range(PHM_N)]
+        for i in range(PHM_N):
+            for b in range(PHM_N):
+                acc = mix_ref[(i * PHM_N + 0) * PHM_N + b] * pieces[0]
+                for a in range(1, PHM_N):
+                    acc = acc + mix_ref[(i * PHM_N + a) * PHM_N + b] * pieces[a]
+                lo = i * 2 * HEAD_DIM + half * HEAD_DIM
+                mixed[b * ROWS : (b + 1) * ROWS, lo : lo + HEAD_DIM] = acc.astype(jnp.bfloat16)
+
+    own_copy.wait()
+    x_of_c = (c_peer + 2) % 4
+    for off in range(1, ctx):
+        shard = (d + off) % ctx
+        w_arrived(shard, c_peer)
+        w_arrived(shard, x_of_c)
+
+    cols_phm = w_ref.shape[1]
+    tile = 256
+    for c in range(cols_phm // tile):
+        weights = wbuf[:, :, c * tile : (c + 1) * tile].reshape(ctx * ROWS, tile)
+        res = jnp.dot(mixed[...], weights, preferred_element_type=jnp.float32)
+        res = res.astype(jnp.bfloat16)
+        for b in range(PHM_N):
+            at = b * cols_phm + c * tile
+            out_ref[:, at : at + tile] = res[b * ROWS : (b + 1) * ROWS]
+
+    for off in range(1, ctx):
+        for j in range(3):
+            head_copy(j, (d + off) % ctx).wait_send()
+    for b in range(ctx):
+
+        @pl.when(d != b)
+        def _():
+            o_copy(b).wait_send()
+
+    @pl.when(z < 3)
+    def _():
+        w_sent(d, r, 0)
+
+    @pl.when(z > 0)
+    def _():
+        w_sent(d, r, 1)
+
+    w_sent(d, r, 2)
+    for k in range(1, 4):
+
+        @pl.when(z - k >= 0)
+        def _():
+            shard = d - 2 * k
+
+            @pl.when(z < 3)
+            def _():
+                w_sent(shard, r, 0)
+
+            w_sent(shard, r, 2)
+
+        @pl.when(z + k <= 3)
+        def _():
+            shard = d + 2 * k
+
+            @pl.when(z > 0)
+            def _():
+                w_sent(shard, r, 1)
+
+            w_sent(shard, r, 2)
+
+    for off in range(1, ctx):
+        shard = (d + off) % ctx
+        w_sent(shard, r, 3)
+        w_sent(shard, r, 4)
+        w_sent(shard, x_peer, 4)
+
+
+def fused_body(queries, key_rows, value_rows, doc_blocks, phm_mix, phm_blocks):
+    ctx = 8
+    any_space = pl.BlockSpec(memory_space=pl.ANY)
+    smem = pl.BlockSpec(memory_space=pltpu.SMEM)
+    cols_phm = phm_blocks.shape[1]
+    return pl.pallas_call(
+        fused_kernel,
+        out_shape=jax.ShapeDtypeStruct((ROWS, PHM_N * cols_phm), jnp.bfloat16),
+        in_specs=[smem, smem, any_space, any_space, any_space, any_space],
+        out_specs=pl.BlockSpec(memory_space=pltpu.VMEM),
+        scratch_shapes=[
+            pltpu.VMEM((3, ctx, ROWS, HEAD_DIM), jnp.bfloat16),
+            pltpu.VMEM((ctx, ROWS, HEAD_DIM), jnp.bfloat16),
+            pltpu.VMEM((ctx, ROWS, HEAD_DIM), jnp.bfloat16),
+            pltpu.VMEM((ctx, ROWS, cols_phm), jnp.bfloat16),
+            pltpu.VMEM((PHM_N * ROWS, ctx * ROWS), jnp.bfloat16),
+            pltpu.SemaphoreType.DMA((3, ctx)),
+            pltpu.SemaphoreType.DMA((3, ctx)),
+            pltpu.SemaphoreType.DMA((ctx,)),
+            pltpu.SemaphoreType.DMA((ctx,)),
+            pltpu.SemaphoreType.DMA((5, ctx, 4)),
+            pltpu.SemaphoreType.DMA((ctx, 4)),
+            pltpu.SemaphoreType.DMA,
+        ],
+        compiler_params=pltpu.CompilerParams(
+            collective_id=0, has_side_effects=True, vmem_limit_bytes=40 * 1024 * 1024
+        ),
+        cost_estimate=pl.CostEstimate(
+            flops=1_600_000_000, bytes_accessed=8_000_000, transcendentals=500_000
+        ),
+    )(doc_blocks, phm_mix.reshape(-1), queries, key_rows, value_rows, phm_blocks)
+
+
+def either_body(sizes, *args):
+    heads = args[0].shape[1] // HEAD_DIM
+    if sizes == (8, 4) and heads == 8 and args[0].shape[0] == ROWS and args[5].shape[0] == ROWS:
+        return fused_body(*args)
+    return body(*args)
+
+
 def solution(mesh):
     placed = (
         P(("rep", "ctx"), None),
@@ -105,6 +411,11 @@
         P(),
         P("ctx", None),
     )
+    sizes = (mesh.shape["ctx"], mesh.shape["rep"])
     return jax.shard_map(
-        body, mesh=mesh, in_specs=placed, out_specs=P(("rep", "ctx"), None), check_vma=False
+        functools.partial(either_body, sizes),
+        mesh=mesh,
+        in_specs=placed,
+        out_specs=P(("rep", "ctx"), None),
+        check_vma=False,
     )

time: 115 us -> 51.4 us (0.45)
  the two profiles are of different devices: /device:TPU:0 before, /device:TPU:1 now
where the time goes in v1:
time: 51.4 us; the launch traced here: 51.1 us
  Pallas kernels  44.7 us (87%)
  local copies, waits for them, and re-layouts  6.32 us (12%)
    pallas_call x1, Pallas kernels, fused_body(): pl.pallas_call(fused_kernel, out_shape=jax.ShapeDtypeStruct((ROWS, PHM_N...  44.7 us
    unnamed x11, local copies, waits for them, and re-layouts  5.53 us

profile of v1, /device:TPU:1, one launch (start us, length us, event | category | flops | bytes accessed | tf_op | source)
XLA Modules:
  0.0 51.1 jit_solution(9762108953750829388)
XLA Ops:
  0.0 0.8 %reshape.3.mix_ref = f32[64]{0:T(128)S(1)} reshape(f32[4,4,4]{2,1,0:T(4,128)} %param.10) | data formatting | bytes 512 | tf_op jit(solution)/shard_map/reshape | solution.py:395
  0.8 0.0 copy-start
  0.8 1.0 %copy-done = bf16[128,1280]{1,0:T(8,128)(2,1)S(1)} copy-done((bf16[128,1280]{1,0:T(8,128)(2,1)S(1)}, bf16[128,1280]{1,0:T(8,128)(2,1)}, u32[]{:S(2)}) %copy-start) | copy-done | bytes 327704
  1.8 0.0 copy-start.1
  1.8 0.9 %copy-done.1 = bf16[128,1024]{1,0:T(8,128)(2,1)S(1)} copy-done((bf16[128,1024]{1,0:T(8,128)(2,1)S(1)}, bf16[128,1024]{1,0:T(8,128)(2,1)}, u32[]{:S(2)}) %copy-start.1) | copy-done | bytes 262168
  2.7 0.0 copy-start.2
  2.7 0.9 %copy-done.2 = bf16[128,1024]{1,0:T(8,128)(2,1)S(1)} copy-done((bf16[128,1024]{1,0:T(8,128)(2,1)S(1)}, bf16[128,1024]{1,0:T(8,128)(2,1)}, u32[]{:S(2)}) %copy-start.2) | copy-done | bytes 262168
  3.7 0.0 copy-start.3
  3.7 0.9 %copy-done.3 = bf16[128,1024]{1,0:T(8,128)(2,1)S(1)} copy-done((bf16[128,1024]{1,0:T(8,128)(2,1)S(1)}, bf16[128,1024]{1,0:T(8,128)(2,1)}, u32[]{:S(2)}) %copy-start.3) | copy-done | bytes 262168
  4.6 0.0 copy-start.4
  4.6 0.7 %copy-done.4 = s32[3]{0:T(128)S(1)} copy-done((s32[3]{0:T(128)S(1)}, s32[3]{0:T(128)}, u32[]{:S(2)}) %copy-start.4) | copy-done | bytes 36
  5.3 44.7 %shard_map.64 = bf16[128,5120]{1,0:T(8,128)(2,1)S(1)} custom-call(s32[3]{0:T(128)S(1)} %copy-done.4, f32[64]{0:T(128)S(1)} %reshape.3.mix_ref, bf16[128,1024]{1,0:T(8,128)(2,1)S(1)} %copy-done.1, bf16[128,1024]{1,0:T(8,128)(2,1)S(1)} %copy-done.2, bf16[128,1024]{1,0:T(8,128)(2,1)S(1)} %copy-done.3, bf16[128,1280]{1,0:T(8,128)(2,1)S(1)} %copy-done), custom_call_target="tpu_custom_call" | custom-call | flops 1600000000 | bytes 8000000 | tf_op jit(solution)/shard_map/pallas_call | solution.py:370
  50.0 1.1 %copy.8 = bf16[128,5120]{1,0:T(8,128)(2,1)} copy(bf16[128,5120]{1,0:T(8,128)(2,1)S(1)} %shard_map.64) | data formatting | bytes 2621440
Async XLA Ops:
  0.8 1.0 %copy-start = (bf16[128,1280]{1,0:T(8,128)(2,1)S(1)}, bf16[128,1280]{1,0:T(8,128)(2,1)}, u32[]{:S(2)}) copy-start(bf16[128,1280]{1,0:T(8,128)(2,1)} %w_ref.1) | copy-start | bytes 983044
  1.8 0.9 %copy-start.1 = (bf16[128,1024]{1,0:T(8,128)(2,1)S(1)}, bf16[128,1024]{1,0:T(8,128)(2,1)}, u32[]{:S(2)}) copy-start(bf16[128,1024]{1,0:T(8,128)(2,1)} %q_ref.1) | copy-start | bytes 786436
  2.7 0.9 %copy-start.2 = (bf16[128,1024]{1,0:T(8,128)(2,1)S(1)}, bf16[128,1024]{1,0:T(8,128)(2,1)}, u32[]{:S(2)}) copy-start(bf16[128,1024]{1,0:T(8,128)(2,1)} %k_ref.1) | copy-start | bytes 786436
  3.7 0.9 %copy-start.3 = (bf16[128,1024]{1,0:T(8,128)(2,1)S(1)}, bf16[128,1024]{1,0:T(8,128)(2,1)}, u32[]{:S(2)}) copy-start(bf16[128,1024]{1,0:T(8,128)(2,1)} %v_ref.1) | copy-start | bytes 786436
  4.6 0.7 %copy-start.4 = (s32[3]{0:T(128)S(1)}, s32[3]{0:T(128)}, u32[]{:S(2)}) copy-start(s32[3]{0:T(128)} %docs_ref.1) | copy-start | bytes 40

commit v2 on v1

--- a/solution.py
+++ b/solution.py
@@ -80,7 +80,9 @@
     )
     seq_len = q_all.shape[0]
     lengths = doc_blocks * UNIT
-    ends = jnp.cumsum(lengths)
+    docs = lengths.shape[0]
+    upto = jnp.arange(docs)[None, :] <= jnp.arange(docs)[:, None]
+    ends = jnp.sum(jnp.where(upto, lengths[None, :], 0), axis=1)
     positions = jnp.arange(seq_len, dtype=jnp.int32)
     doc_ids = jnp.sum((positions[:, None] >= ends[None, :]).astype(jnp.int32), axis=1)
     attended = attend(q_all, k_all, v_all, doc_ids)
@@ -106,27 +108,40 @@
 
 def fused_kernel(
     docs_ref, mix_ref, q_ref, k_ref, v_ref, w_ref, out_ref,
-    qkv, obuf, att, wbuf, mixed,
-    qkv_send, qkv_recv, o_send, o_recv, w_send, w_recv, own_sem,
+    qh, kv, obuf, att, wbuf, mixed,
+    q_send, q_recv, kv_send, kv_recv, o_send, o_recv, w_send, w_recv, own_sem,
 ):
     ctx = 8
     window = 4
     d = lax.axis_index("ctx")
     r = lax.axis_index("rep")
     z = d // 2
+    p = d % 2
+    half_heads = 4
+    half_cols = half_heads * HEAD_DIM
     y_peer = d + 1 - 2 * (d % 2)
     x_peer = (r + 2) % 4
     c_peer = r + 1 - 2 * (r % 2)
     part = ROWS // 4
 
     barrier = pltpu.get_barrier_semaphore()
-    for off in range(1, ctx):
-        pl.semaphore_signal(
-            barrier, inc=1, device_id={"ctx": (d + off) % ctx}, device_id_type=MESH
-        )
-    for peer in (x_peer, c_peer):
-        pl.semaphore_signal(barrier, inc=1, device_id={"rep": peer}, device_id_type=MESH)
-    pl.semaphore_wait(barrier, ctx + 1)
+
+    def greet(target):
+        pl.semaphore_signal(barrier, inc=1, device_id=target, device_id_type=MESH)
+
+    greet({"ctx": y_peer})
+    greet({"rep": x_peer})
+    greet({"rep": c_peer})
+
+    @pl.when(z < 3)
+    def _():
+        greet({"ctx": d + 2})
+
+    @pl.when(z > 0)
+    def _():
+        greet({"ctx": d - 2})
+
+    pl.semaphore_wait(barrier, 4 + jnp.where((z > 0) & (z < 3), 1, 0))
 
     def quarter(shard, which):
         return wbuf.at[shard, pl.ds(pl.multiple_of(which * part, part), part)]
@@ -151,8 +166,50 @@
 
     own_w = w_ref.at[pl.ds(pl.multiple_of(r * part, part), part)]
 
+    refs = (k_ref, v_ref)
+
+    def half_of(ref, which):
+        return ref.at[:, pl.ds(pl.multiple_of(which * half_cols, half_cols), half_cols)]
+
+    def remote(src, dst, send, recv, to):
+        return pltpu.make_async_remote_copy(
+            src_ref=src, dst_ref=dst, send_sem=send, recv_sem=recv,
+            device_id={"ctx": to}, device_id_type=MESH,
+        )
+
+    def kv_partner(j):
+        return remote(
+            half_of(refs[j], 1 - p), kv.at[j, 3 + p], kv_send.at[j, 0], kv_recv.at[j, 3 + p], y_peer
+        )
+
+    def kv_up(j):
+        return remote(
+            half_of(refs[j], p), kv.at[j, 1 + p], kv_send.at[j, 1], kv_recv.at[j, 1 + p], d + 2
+        )
+
+    def kv_relay(j):
+        return remote(
+            kv.at[j, 4 - p], kv.at[j, 2 - p], kv_send.at[j, 2], kv_recv.at[j, 2 - p], d + 2
+        )
+
+    def kv_far(j):
+        return remote(kv.at[j, 2], kv.at[j, 0], kv_send.at[j, 3], kv_recv.at[j, 0], d + 2)
+
+    def kv_here(j, slot):
+        here = kv.at[j, slot]
+        pltpu.make_async_copy(here, here, kv_recv.at[j, slot]).wait()
+
+    q_partner = remote(half_of(q_ref, 1 - p), qh.at[p], q_send, q_recv.at[p], y_peer)
+    for j in range(2):
+        kv_partner(j).start()
+
     @pl.when(z < 3)
     def _():
+        for j in range(2):
+            kv_up(j).start()
+
+    @pl.when(z < 3)
+    def _():
         w_copy(own_w, d, r, 0, {"ctx": d + 2}).start()
 
     @pl.when(z > 0)
@@ -161,29 +218,20 @@
 
     w_copy(own_w, d, r, 2, {"ctx": y_peer}).start()
 
-    refs = (q_ref, k_ref, v_ref)
-
-    def head_copy(j, to):
-        return pltpu.make_async_remote_copy(
-            src_ref=refs[j].at[:, pl.ds(pl.multiple_of(to * HEAD_DIM, HEAD_DIM), HEAD_DIM)],
-            dst_ref=qkv.at[j, d],
-            send_sem=qkv_send.at[j, to],
-            recv_sem=qkv_recv.at[j, d],
-            device_id={"ctx": to},
-            device_id_type=MESH,
-        )
-
-    for off in (4, 5, 3, 6, 2, 7, 1):
-        for j in range(3):
-            head_copy(j, (d + off) % ctx).start()
-    for j in range(3):
-        pltpu.make_async_copy(
-            refs[j].at[:, pl.ds(pl.multiple_of(d * HEAD_DIM, HEAD_DIM), HEAD_DIM)],
-            qkv.at[j, d],
-            qkv_recv.at[j, d],
-        ).start()
+    for j in range(2):
+        pltpu.make_async_copy(half_of(refs[j], p), kv.at[j, 3 + p], kv_recv.at[j, 3 + p]).start()
+    q_partner.start()
+    pltpu.make_async_copy(half_of(q_ref, p), qh.at[p], q_recv.at[p]).start()
     own_copy = pltpu.make_async_copy(w_ref, wbuf.at[d], own_sem)
     own_copy.start()
+
+    @pl.when(z < 1)
+    def _():
+        kv[:, 1:3] = jnp.zeros((2, 2, ROWS, half_cols), jnp.bfloat16)
+
+    @pl.when(z < 2)
+    def _():
+        kv[:, 0:1] = jnp.zeros((2, 1, ROWS, half_cols), jnp.bfloat16)
 
     def forward(shard, which, way, target):
         w_copy(quarter(shard, which), shard, which, way, target).start()
@@ -215,6 +263,24 @@
             forward(shard, r, 2, {"ctx": y_peer})
             forward(shard, r, 3, {"rep": x_peer})
             forward(shard, r, 4, {"rep": c_peer})
+
+    for j in range(2):
+        kv_here(j, 3)
+        kv_here(j, 4)
+
+        @pl.when(z < 3)
+        def _():
+            kv_relay(j).start()
+
+    for j in range(2):
+
+        @pl.when(z > 0)
+        def _():
+            kv_here(j, 2)
+
+        @pl.when((z > 0) & (z < 3))
+        def _():
+            kv_far(j).start()
 
     for k in range(4):
         shard = (y_peer + 2 * k) % ctx
@@ -225,76 +291,76 @@
     ends = [docs_ref[0]]
     for i in range(1, docs_ref.shape[0]):
         ends.append(ends[-1] + docs_ref[i])
-    ids = []
-    for b in range(ctx):
+    factor = math.log2(math.e) / math.sqrt(HEAD_DIM)
+    rows = lax.broadcasted_iota(jnp.int32, (ROWS, ROWS), 0)
+    cols = lax.broadcasted_iota(jnp.int32, (ROWS, ROWS), 1)
+
+    def doc_of(b):
         doc = jnp.int32(0)
         for e in ends:
             doc = doc + jnp.where(e <= b, jnp.int32(1), jnp.int32(0))
-        ids.append(doc)
-    factor = math.log2(math.e) / math.sqrt(HEAD_DIM)
-    rows = lax.broadcasted_iota(jnp.int32, (ROWS, ROWS), 0)
-    cols = lax.broadcasted_iota(jnp.int32, (ROWS, ROWS), 1)
-
-    def o_copy(b):
-        return pltpu.make_async_remote_copy(
-            src_ref=obuf.at[b],
-            dst_ref=att.at[d],
-            send_sem=o_send.at[b],
-            recv_sem=o_recv.at[d],
-            device_id={"ctx": b},
-            device_id_type=MESH,
-        )
-
-    for b in range(ctx):
-        for j in range(3):
-            here = qkv.at[j, b]
-            pltpu.make_async_copy(here, here, qkv_recv.at[j, b]).wait()
-        low = max(0, b - window + 1)
-        wide = (b + 1 - low) * ROWS
-        keys = qkv[1, low : b + 1].reshape(wide, HEAD_DIM)
-        vals = qkv[2, low : b + 1].reshape(wide, HEAD_DIM)
-        scores = lax.dot_general(
-            qkv[0, b], keys, (((1,), (1,)), ((), ())), preferred_element_type=jnp.float32
-        )
-        parts = []
-        for kb in range(low, b + 1):
-            one = scores[:, (kb - low) * ROWS : (kb - low + 1) * ROWS]
-            if kb == b:
-                one = jnp.where(cols <= rows, one, MASKED)
+        return doc
+
+    for j in range(2):
+
+        @pl.when(z > 0)
+        def _():
+            kv_here(j, 1)
+
+        @pl.when(z > 1)
+        def _():
+            kv_here(j, 0)
+
+    for par in range(2):
+        here = qh.at[par]
+        pltpu.make_async_copy(here, here, q_recv.at[par]).wait()
+
+    o_copy = remote(obuf, att.at[pl.ds(half_heads * p, half_heads)], o_send, o_recv, y_peer)
+    wide = window * ROWS
+    for par, own in ((1 - p, False), (p, True)):
+        block = 2 * z + par
+        doc = doc_of(block)
+        bias = []
+        for i in range(window - 1):
+            b = block - (window - 1) + i
+            bias.append(jnp.where((b >= 0) & (doc_of(b) == doc), 0.0, MASKED))
+        for h in range(half_heads):
+            lanes = slice(h * HEAD_DIM, (h + 1) * HEAD_DIM)
+            keys = kv[0, pl.ds(par, window), :, lanes].reshape(wide, HEAD_DIM)
+            vals = kv[1, pl.ds(par, window), :, lanes].reshape(wide, HEAD_DIM)
+            scores = lax.dot_general(
+                qh[par, :, lanes], keys, (((1,), (1,)), ((), ())),
+                preferred_element_type=jnp.float32,
+            )
+            parts = [scores[:, i * ROWS : (i + 1) * ROWS] + bias[i] for i in range(window - 1)]
+            parts.append(jnp.where(cols <= rows, scores[:, (window - 1) * ROWS :], MASKED))
+            masked = jnp.concatenate(parts, axis=1)
+            top = jnp.max(masked, axis=1, keepdims=True)
+            expd = jnp.exp2((masked - top) * factor)
+            total = jnp.sum(expd, axis=1, keepdims=True)
+            got = jnp.dot(expd.astype(jnp.bfloat16), vals, preferred_element_type=jnp.float32)
+            got = (got / total).astype(jnp.bfloat16)
+            if own:
+                att[half_heads * p + h] = got
             else:
-                one = one + jnp.where(ids[kb] == ids[b], 0.0, MASKED)
-            parts.append(one)
-        masked = jnp.concatenate(parts, axis=1) if len(parts) > 1 else parts[0]
-        top = jnp.max(masked, axis=1, keepdims=True)
-        expd = jnp.exp2((masked - top) * factor)
-        total = jnp.sum(expd, axis=1, keepdims=True)
-        got = jnp.dot(expd.astype(jnp.bfloat16), vals, preferred_element_type=jnp.float32)
-        obuf[b] = (got / total).astype(jnp.bfloat16)
-
-        @pl.when(d != b)
-        def _():
-            o_copy(b).start()
-
-        @pl.when(d == b)
-        def _():
-            pltpu.make_async_copy(obuf.at[b], att.at[d], o_recv.at[d]).start()
+                obuf[h] = got
+        if not own:
+            o_copy.start()
 
     for off in range(1, ctx):
         shard = (d + off) % ctx
         w_arrived(shard, x_peer)
         forward(shard, x_peer, 4, {"rep": c_peer})
 
-    for h in range(ctx):
-        here = att.at[h]
-        pltpu.make_async_copy(here, here, o_recv.at[h]).wait()
+    o_copy.wait_recv()
 
     for half in range(2):
         pieces = [att[2 * a + half].astype(jnp.float32) for a in range(PHM_N)]
         for i in range(PHM_N):
             for b in range(PHM_N):
-                acc = mix_ref[(i * PHM_N + 0) * PHM_N + b] * pieces[0]
+                acc = mix_ref[i, 0, b] * pieces[0]
                 for a in range(1, PHM_N):
-                    acc = acc + mix_ref[(i * PHM_N + a) * PHM_N + b] * pieces[a]
+                    acc = acc + mix_ref[i, a, b] * pieces[a]
                 lo = i * 2 * HEAD_DIM + half * HEAD_DIM
                 mixed[b * ROWS : (b + 1) * ROWS, lo : lo + HEAD_DIM] = acc.astype(jnp.bfloat16)
 
@@ -315,14 +381,19 @@
             at = b * cols_phm + c * tile
             out_ref[:, at : at + tile] = res[b * ROWS : (b + 1) * ROWS]
 
-    for off in range(1, ctx):
-        for j in range(3):
-            head_copy(j, (d + off) % ctx).wait_send()
-    for b in range(ctx):
-
-        @pl.when(d != b)
-        def _():
-            o_copy(b).wait_send()
+    q_partner.wait_send()
+    o_copy.wait_send()
+    for j in range(2):
+        kv_partner(j).wait_send()
+
+        @pl.when(z < 3)
+        def _():
+            kv_up(j).wait_send()
+            kv_relay(j).wait_send()
+
+        @pl.when((z > 0) & (z < 3))
+        def _():
+            kv_far(j).wait_send()
 
     @pl.when(z < 3)
     def _():
@@ -373,26 +444,29 @@
         in_specs=[smem, smem, any_space, any_space, any_space, any_space],
         out_specs=pl.BlockSpec(memory_space=pltpu.VMEM),
         scratch_shapes=[
-            pltpu.VMEM((3, ctx, ROWS, HEAD_DIM), jnp.bfloat16),
-            pltpu.VMEM((ctx, ROWS, HEAD_DIM), jnp.bfloat16),
+            pltpu.VMEM((2, ROWS, 4 * HEAD_DIM), jnp.bfloat16),
+            pltpu.VMEM((2, 5, ROWS, 4 * HEAD_DIM), jnp.bfloat16),
+            pltpu.VMEM((4, ROWS, HEAD_DIM), jnp.bfloat16),
             pltpu.VMEM((ctx, ROWS, HEAD_DIM), jnp.bfloat16),
             pltpu.VMEM((ctx, ROWS, cols_phm), jnp.bfloat16),
             pltpu.VMEM((PHM_N * ROWS, ctx * ROWS), jnp.bfloat16),
-            pltpu.SemaphoreType.DMA((3, ctx)),
-            pltpu.SemaphoreType.DMA((3, ctx)),
-            pltpu.SemaphoreType.DMA((ctx,)),
-            pltpu.SemaphoreType.DMA((ctx,)),
+            pltpu.SemaphoreType.DMA,
+            pltpu.SemaphoreType.DMA((2,)),
+            pltpu.SemaphoreType.DMA((2, 4)),
+            pltpu.SemaphoreType.DMA((2, 5)),
+            pltpu.SemaphoreType.DMA,
+            pltpu.SemaphoreType.DMA,
             pltpu.SemaphoreType.DMA((5, ctx, 4)),
             pltpu.SemaphoreType.DMA((ctx, 4)),
             pltpu.SemaphoreType.DMA,
         ],
         compiler_params=pltpu.CompilerParams(
-            collective_id=0, has_side_effects=True, vmem_limit_bytes=40 * 1024 * 1024
+            collective_id=0, has_side_effects=True, vmem_limit_bytes=60 * 1024 * 1024
         ),
         cost_estimate=pl.CostEstimate(
             flops=1_600_000_000, bytes_accessed=8_000_000, transcendentals=500_000
         ),
-    )(doc_blocks, phm_mix.reshape(-1), queries, key_rows, value_rows, phm_blocks)
+    )(doc_blocks, phm_mix, queries, key_rows, value_rows, phm_blocks)
 
 
 def either_body(sizes, *args):

time: 51.4 us -> 40.2 us (0.78)
  the two profiles are of different devices: /device:TPU:1 before, /device:TPU:26 now
where the time goes in v2:
time: 40.2 us; the launch traced here: 40 us
  Pallas kernels  37.6 us (94%)
  local copies, waits for them, and re-layouts  2.46 us (6%)
    pallas_call x1, Pallas kernels, fused_body(): pl.pallas_call(fused_kernel, out_shape=jax.ShapeDtypeStruct((ROWS, PHM_N...  37.6 us
    unnamed x1, local copies, waits for them, and re-layouts  2.46 us

profile of v2, /device:TPU:26, one launch (start us, length us, event | category | flops | bytes accessed | tf_op | source)
XLA Modules:
  0.0 40.0 jit_solution(16162035320869070781)
XLA Ops:
  0.0 37.6 %shard_map.64 = bf16[128,5120]{1,0:T(8,128)(2,1)} custom-call(s32[3]{0:T(128)} %docs_ref.1, f32[4,4,4]{2,1,0:T(4,128)} %mix_ref.1, bf16[128,1024]{1,0:T(8,128)(2,1)} %q_ref.1, bf16[128,1024]{1,0:T(8,128)(2,1)} %k_ref.1, bf16[128,1024]{1,0:T(8,128)(2,1)} %v_ref.1, bf16[128,1280]{1,0:T(8,128)(2,1)} %w_ref.1), custom_call_target="tpu_custom_call" | custom-call | flops 1600000000 | bytes 8000000 | tf_op jit(solution)/shard_map/pallas_call | solution.py:441
  37.6 2.5 %copy.8 = bf16[128,5120]{1,0:T(8,128)(2,1)} copy(bf16[128,5120]{1,0:T(8,128)(2,1)} %shard_map.64) | data formatting | bytes 2621440

commit v3 on v2

--- a/solution.py
+++ b/solution.py
@@ -200,6 +200,16 @@
         pltpu.make_async_copy(here, here, kv_recv.at[j, slot]).wait()
 
     q_partner = remote(half_of(q_ref, 1 - p), qh.at[p], q_send, q_recv.at[p], y_peer)
+    @pl.when(z < 3)
+    def _():
+        w_copy(own_w, d, r, 0, {"ctx": d + 2}).start()
+
+    @pl.when(z > 0)
+    def _():
+        w_copy(own_w, d, r, 1, {"ctx": d - 2}).start()
+
+    w_copy(own_w, d, r, 2, {"ctx": y_peer}).start()
+
     for j in range(2):
         kv_partner(j).start()
 
@@ -207,16 +217,6 @@
     def _():
         for j in range(2):
             kv_up(j).start()
-
-    @pl.when(z < 3)
-    def _():
-        w_copy(own_w, d, r, 0, {"ctx": d + 2}).start()
-
-    @pl.when(z > 0)
-    def _():
-        w_copy(own_w, d, r, 1, {"ctx": d - 2}).start()
-
-    w_copy(own_w, d, r, 2, {"ctx": y_peer}).start()
 
     for j in range(2):
         pltpu.make_async_copy(half_of(refs[j], p), kv.at[j, 3 + p], kv_recv.at[j, 3 + p]).start()

time: 40.2 us -> 39.4 us (0.980)
  Pallas kernels: 37.6 us -> 36.7 us
    pallas_call x1, Pallas kernels: 37.6 us -> 36.7 us  [fused_body(): pl.pallas_call(fused_kernel, out_shape=jax.ShapeDtypeStruct((ROWS, PHM_N...]
where the time goes in v3:
time: 39.4 us; the launch traced here: 39.2 us
  Pallas kernels  36.7 us (93%)
  local copies, waits for them, and re-layouts  2.46 us (6%)
    pallas_call x1, Pallas kernels, fused_body(): pl.pallas_call(fused_kernel, out_shape=jax.ShapeDtypeStruct((ROWS, PHM_N...  36.7 us
    unnamed x1, local copies, waits for them, and re-layouts  2.46 us

profile of v3, /device:TPU:26, one launch (start us, length us, event | category | flops | bytes accessed | tf_op | source)
XLA Modules:
  0.0 39.2 jit_solution(10952927350097032407)
XLA Ops:
  0.0 36.7 %shard_map.64 = bf16[128,5120]{1,0:T(8,128)(2,1)} custom-call(s32[3]{0:T(128)} %docs_ref.1, f32[4,4,4]{2,1,0:T(4,128)} %mix_ref.1, bf16[128,1024]{1,0:T(8,128)(2,1)} %q_ref.1, bf16[128,1024]{1,0:T(8,128)(2,1)} %k_ref.1, bf16[128,1024]{1,0:T(8,128)(2,1)} %v_ref.1, bf16[128,1280]{1,0:T(8,128)(2,1)} %w_ref.1), custom_call_target="tpu_custom_call" | custom-call | flops 1600000000 | bytes 8000000 | tf_op jit(solution)/shard_map/pallas_call | solution.py:441
  36.7 2.5 %copy.8 = bf16[128,5120]{1,0:T(8,128)(2,1)} copy(bf16[128,5120]{1,0:T(8,128)(2,1)} %shard_map.64) | data formatting | bytes 2621440
